TPU v7x, 32 devices: a whole 2x2x4 slice. The times are simulated.
32 devices in a mesh: req: 16 (over z, y, core), head: 2 (over x).
Axes of the slice: x: 2, y: 2, z: 4, core: 2. Of those that a mesh axis runs over, the one named last changes fastest.
Arguments:
- queries: bfloat16 [64, 8192], P('req', 'head'), may hold values from -200 to 200
- new_kv: bfloat16 [2, 64, 1024], P(None, 'req', 'head'), may hold values from -6 to 6
- own_kv: bfloat16 [2, 512, 64, 1024], P(None, 'req', None, 'head'), may hold values from -6 to 6
- man_kv: bfloat16 [2, 32, 64, 1024], P(None, 'req', None, 'head'), may hold values from -6 to 6
- pages: int32 [64, 8], P('req'), may hold values from 0 to 31
- own_len: int32 [64], P('req'), may hold values from 1 to 8, as said below
- resid: bfloat16 [64, 8192], P(None, 'req'), may hold values from -3 to 3
- w_out: bfloat16 [8192, 8192], P('head', 'req'), may hold values from -0.8984375 to 0.8984375
- w_gate: bfloat16 [8192, 14336], P('req', 'head'), may hold values from -0.0625 to 0.0625
- w_up: bfloat16 [8192, 14336], P('req', 'head'), may hold values from -0.0625 to 0.0625
Outputs:
- resid_out: bfloat16 [64, 8192], P(None, 'req')
- hidden: bfloat16 [64, 14336], P('req', 'head')
Inputs may be any that keep to these rules, and one draw needn't show every extreme that they name: `pages`: entries at and past a request's length are padding. `own_len`: among the 4 requests of each index of req one has 8 pages.
All inputs are finite; a program needn't handle non-finite values.
Results may differ from a plain program's by a relative error of at most 0.03.
Values may be sent and summed in bfloat16 or wider, within the bound.
A program may use at most 64 MiB of HBM per device.

v0:
```python
import jax
import jax.numpy as jnp
from jax import lax
from jax.sharding import PartitionSpec as P

HD = 128
PAGE = 64
MAXP = 8
GROUP = 8


def block_scores(query_matrix, keys):
    return jnp.einsum(
        "bkgd,tkd->bkgt", query_matrix, keys, preferred_element_type=jnp.float32
    ) * HD ** (-0.5)


def fold_block(carry, scores, values):
    top, total, acc = carry
    new_top = jnp.maximum(top, scores.max(-1))
    factor = jnp.exp(top - new_top)
    weights = jnp.exp(scores - new_top[..., None])
    total = total * factor + weights.sum(-1)
    acc = acc * factor[..., None] + jnp.einsum(
        "bkgt,tkd->bkgd", weights.astype(jnp.bfloat16), values, preferred_element_type=jnp.float32
    )
    return (new_top, total, acc)


def on_device(queries, new_kv, own_kv, man_kv, pages, own_len, resid, w_out, w_gate, w_up):
    rows = queries.shape[0]
    kv_dev = new_kv.shape[2] // HD
    query_matrix = queries.reshape(rows, kv_dev, GROUP, HD)
    picked = own_kv[:, pages].reshape(2, rows, MAXP * PAGE, kv_dev, HD)
    valid = jnp.repeat(jnp.arange(MAXP, dtype=jnp.int32)[None, :] < own_len[:, None], PAGE, axis=1)
    s_own = jnp.einsum(
        "bkgd,btkd->bkgt", query_matrix, picked[0], preferred_element_type=jnp.float32
    ) * HD ** (-0.5)
    s_own = jnp.where(valid[:, None, None, :], s_own, -jnp.inf)
    newest_token = new_kv.reshape(2, rows, kv_dev, HD)
    s_new = jnp.einsum(
        "slea,sla->sle", query_matrix, newest_token[0], preferred_element_type=jnp.float32
    ) * HD ** (-0.5)
    top = jnp.maximum(s_own.max(-1), s_new)
    w_own = jnp.exp(s_own - top[..., None])
    newest_weight = jnp.exp(s_new - top)
    total = w_own.sum(-1) + newest_weight
    acc = jnp.einsum(
        "bkgt,btkd->bkgd", w_own.astype(jnp.bfloat16), picked[1], preferred_element_type=jnp.float32
    )
    acc = acc + jnp.einsum(
        "acy,acx->acyx",
        newest_weight.astype(jnp.bfloat16),
        newest_token[1],
        preferred_element_type=jnp.float32,
    )
    carry = (top, total, acc)
    piece = lax.all_gather(man_kv, "req", axis=1, tiled=True)
    keys = piece[0].reshape(-1, kv_dev, HD)
    values = piece[1].reshape(-1, kv_dev, HD)
    top, total, acc = fold_block(carry, block_scores(query_matrix, keys), values)
    attn = (acc / total[..., None]).astype(jnp.bfloat16).reshape(rows, kv_dev * GROUP * HD)
    partial_out = jnp.dot(
        lax.all_gather(attn, "req", axis=0, tiled=True), w_out, preferred_element_type=jnp.float32
    )
    summed = lax.psum(partial_out.astype(jnp.bfloat16), "head").astype(jnp.float32)
    resid_out = (resid.astype(jnp.float32) + summed).astype(jnp.bfloat16)
    gate_part = jnp.dot(resid_out, w_gate, preferred_element_type=jnp.float32)
    up_projection_piece = jnp.dot(resid_out, w_up, preferred_element_type=jnp.float32)
    joined = lax.psum_scatter(
        jnp.concatenate([gate_part, up_projection_piece], axis=1),
        "req",
        scatter_dimension=0,
        tiled=True,
    )
    width = w_gate.shape[1]
    hidden = (jax.nn.silu(joined[:, :width]) * joined[:, width:]).astype(jnp.bfloat16)
    return (resid_out, hidden)


def solution(mesh):
    in_specs = (
        P("req", "head"),
        P(None, "req", "head"),
        P(None, "req", None, "head"),
        P(None, "req", None, "head"),
        P("req", None),
        P("req"),
        P(None, "req"),
        P("head", "req"),
        P("req", "head"),
        P("req", "head"),
    )
    out_specs = (P(None, "req"), P("req", "head"))
    return jax.shard_map(
        on_device, mesh=mesh, in_specs=in_specs, out_specs=out_specs, check_vma=False
    )
```

profile of v0, /device:TPU:0, one launch (start us, length us, event | category | flops | bytes accessed | tf_op | source)
XLA Modules:
  0.0 246.8 jit_solution(8915186866605371468)
XLA Ops:
  7.2 0.7 all-gather.3.cloned.1.call-update
  7.9 0.7 compare_select_fusion
  8.6 0.1 reshape.36
  8.7 5.0 %gather_fusion = bf16[32,2,64,512]{3,2,1,0:T(8,128)(2,1)} fusion(bf16[2,32,64,512]{3,2,1,0:T(8,128)(2,1)} %param.12, s32[1024]{0:T(1024)S(1)} %pad_clamp_fusion), kind=kCustom, calls=%fused_computation | custom fusion | bytes 8388736 | tf_op jit(solution)/shard_map/gather | solution.py:34
  13.7 2.7 %copy.104 = bf16[4,8,2,64,512]{4,3,1,0,2:T(8,128)(2,1)S(1)} copy(bf16[4,8,2,64,512]{4,3,2,1,0:T(8,128)(2,1)} %bitcast.50) | data formatting | bytes 8388608 | tf_op jit(solution)/shard_map/gather | solution.py:34
  16.4 1.7 fusion.46
  18.1 4.1 %squeeze.10 = bf16[4,512,4,128]{3,2,1,0:T(4,128)(2,1)} reshape(bf16[1,4,8,64,512]{4,3,2,1,0:T(8,128)(2,1)} %get-tuple-element.5) | data formatting | bytes 4194304 | tf_op jit(solution)/shard_map/squeeze | solution.py:37
  22.4 0.1 broadcast_in_dim.27
  22.5 2.1 squeeze.12
  24.6 0.1 fusion.50
  24.7 2.3 fusion.48
  27.1 0.2 fusion.39
  27.3 36.2 %all-gather.3.cloned.1.call-done = bf16[2,32,64,512]{3,2,1,0:T(8,128)(2,1)} async-done(((bf16[2,2,64,512]{3,2,1,0:T(8,128)(2,1)}), bf16[2,32,64,512]{3,2,1,0:T(8,128)(2,1)}) %all-gather.3.cloned.1.call-update) | async-done | bytes 4194320 | tf_op jit(solution)/shard_map/all_gather | solution.py:58
  63.5 4.0 %fusion.47 = (bf16[1,32,64,512]{3,2,1,0:T(8,128)(2,1)}, bf16[1,32,64,512]{3,2,1,0:T(8,128)(2,1)S(1)}) fusion(bf16[2,32,64,512]{3,2,1,0:T(8,128)(2,1)} %all-gather.3.cloned.1.call-done), kind=kLoop, calls=%fused_computation.48 | loop fusion | bytes 8388608 | tf_op jit(solution)/shard_map/slice | solution.py:59
  67.5 4.0 %reshape_squeeze.6 = bf16[2048,4,128]{2,1,0:T(4,128)(2,1)} reshape(bf16[1,32,64,512]{3,2,1,0:T(8,128)(2,1)} %get-tuple-element.6) | data formatting | bytes 4194304 | tf_op jit(solution)/shard_map/reshape;squeeze | solution.py:59
  71.4 2.5 fusion.49
  73.9 2.1 reshape_squeeze.7
  76.0 0.3 fusion.36
  76.3 2.2 fusion.30
  78.5 0.5 fusion.33
  79.0 20.3 %all-gather = bf16[16,4,4096]{2,1,0:T(4,128)(2,1)S(1)} all-gather(bf16[1,4,4096]{2,1,0:T(4,128)(2,1)S(1)} %reshape.44), channel_id=1, replica_groups=mesh['req'=16,'head'=2] {'req'}, dimensions={0}, use_global_device_ids=true | all-gather | bytes 557056 | tf_op jit(solution)/shard_map/all_gather | solution.py:64
  99.4 0.9 reshape.45
  100.3 4.0 %convolution_convert_fusion = bf16[64,512]{1,0:T(8,128)(2,1)} fusion(bf16[64,4096]{1,0:T(8,128)(2,1)} %reshape.45, bf16[4096,512]{1,0:T(8,128)(2,1)} %param.17), kind=kOutput, calls=%fused_computation.16 | convolution fusion | flops 268468224 | bytes 4784128 | tf_op jit(solution)/shard_map/dot_general | solution.py:63
  104.3 18.1 %all-reduce.4.cloned.1.call-done = bf16[64,512]{1,0:T(8,128)(2,1)} async-done(((bf16[64,512]{1,0:T(8,128)(2,1)}), bf16[64,512]{1,0:T(8,128)(2,1)}) %all-reduce.4.cloned.1.call-update) | async-done | bytes 65552 | tf_op jit(solution)/shard_map/psum | solution.py:66
  122.5 0.9 add_convert_fusion
  123.3 4.6 %fusion.51 = f32[64,7168]{1,0:T(8,128)S(1)} fusion(bf16[64,512]{1,0:T(8,128)(2,1)S(1)} %add_convert_fusion, bf16[512,7168]{1,0:T(8,128)(2,1)} %param.18), kind=kOutput, calls=%fused_computation.52 | convolution fusion | flops 469762048 | bytes 9240576 | tf_op jit(solution)/shard_map/dot_general | solution.py:68
  128.0 1.4 fusion.52
  129.4 2.1 pad_maximum_fusion
  131.5 0.6 copy-done.6
  132.1 0.6 dynamic-slice
  133.3 105.1 %all-reduce.6.cloned.1.call-done = f32[64,14336]{1,0:T(8,128)} async-done(((f32[64,14336]{1,0:T(8,128)}), f32[64,14336]{1,0:T(8,128)}) %all-reduce.6.cloned.1.call-update) | async-done | bytes 3670032
  238.5 1.8 fusion.44
  (34 shorter events, 0.5 us)
Async XLA Ops:
  7.2 56.3 %all-gather.3.cloned.1.call-start = ((), (), s32[]{:S(2)}) async-start(), calls=%async_computation | async-start | bytes 4456448 | tf_op jit(solution)/shard_map/all_gather | solution.py:58
  7.9 114.6 %all-reduce.4.cloned.1.call-start = ((), (), s32[]{:S(2)}) async-start(), calls=%async_computation.1 | async-start | bytes 131072 | tf_op jit(solution)/shard_map/psum | solution.py:66
  18.1 4.1 %copy-start.5 = (s32[4]{0:T(128)S(1)}, s32[4]{0:T(128)}, u32[]{:S(2)}) copy-start(s32[4]{0:T(128)} %param.15) | copy-start | bytes 52
  18.1 4.3 %copy-start.3 = (bf16[2,4,512]{2,1,0:T(4,128)(2,1)S(1)}, bf16[2,4,512]{2,1,0:T(4,128)(2,1)}, u32[]{:S(2)}) copy-start(bf16[2,4,512]{2,1,0:T(4,128)(2,1)} %param.11) | copy-start | bytes 24580
  22.5 2.1 copy-start.4
  76.0 2.5 %copy-start = (bf16[4,512,4,128]{3,2,1,0:T(4,128)(2,1)S(1)}, bf16[4,512,4,128]{3,2,1,0:T(4,128)(2,1)}, u32[]{:S(2)}) copy-start(bf16[4,512,4,128]{3,2,1,0:T(4,128)(2,1)} %squeeze.12) | copy-start | bytes 6291460
  100.3 22.2 %copy-start.2 = (bf16[64,512]{1,0:T(8,128)(2,1)S(1)}, bf16[64,512]{1,0:T(8,128)(2,1)}, u32[]{:S(2)}) copy-start(bf16[64,512]{1,0:T(8,128)(2,1)} %param.16) | copy-start | bytes 196612
  100.3 27.7 %slice-start = ((s8[7340032]{0:T(1024)(128)(4,1)}), s8[3145728]{0:T(1024)(128)(4,1)S(1)}, s32[]{:S(2)}) async-start(s8[7340032]{0:T(1024)(128)(4,1)} %bitcast.52), calls=%async_computation.3 | async-start | bytes 6291456
  104.3 134.2 %all-reduce.6.cloned.1.call-start = ((), (), s32[]{:S(2)}) async-start(), calls=%async_computation.2 | async-start | bytes 7340032
  123.3 4.7 %copy-start.1 = (bf16[64,512]{1,0:T(8,128)(2,1)}, bf16[64,512]{1,0:T(8,128)(2,1)S(1)}, u32[]{:S(2)}) copy-start(bf16[64,512]{1,0:T(8,128)(2,1)S(1)} %add_convert_fusion) | copy-start | bytes 196612
  123.3 4.7 %slice-start.1 = ((s8[7340032]{0:T(1024)(128)(4,1)}), s8[4194304]{0:T(1024)(128)(4,1)S(1)}, s32[]{:S(2)}) async-start(s8[7340032]{0:T(1024)(128)(4,1)} %bitcast.52), calls=%async_computation.4 | async-start | bytes 8388608
  131.5 0.7 copy-start.6
Sparse Core Ops, SparseCore 0:
  10.2 53.2 all-gather.2
  104.4 18.0 all-reduce.3
  131.6 106.8 all-reduce.5
where the time goes:
time: 247 us
  waiting for transfers between devices  160 us (65%)
  local copies, waits for them, and re-layouts  28 us (11%)
  blocking collectives  20.3 us (8%)
  matrix products  17.6 us (7%)
  between operations  14.5 us (6%)
  other arithmetic  6.04 us (2%)
    unnamed x4, waiting for transfers between devices  106 us
    all_gather x1, waiting for transfers between devices, on_device(): piece = lax.all_gather(man_kv, 'req', axis=1, tiled=True)  36.2 us
    all_gather x1, blocking collectives, on_device(): lax.all_gather(attn, 'req', axis=0, tiled=True)  20.3 us
    psum x1, waiting for transfers between devices, on_device(): lax.psum(partial_out.astype(jnp.bfloat16), 'head').astype(jnp.float32)  18.1 us
    gather x2, local copies, waits for them, and re-layouts, on_device(): picked = own_kv[:, pages].reshape(2, rows, MAXP * PAGE, kv_dev, HD)  7.65 us
  transfers between devices with their start and end apart: 3, of which 3 were waited for; matrix products, arithmetic and copies ran while one was open for 8% of the time, Pallas kernels for 0%

commit v1 on v0

v1 whole, which is shorter than its diff:
```python
import functools

import jax
import jax.numpy as jnp
from jax import lax
from jax.experimental import pallas as pl
from jax.experimental.pallas import tpu as pltpu
from jax.sharding import PartitionSpec as P

HD = 128
PAGE = 64
MAXP = 8
GROUP = 8
CORES = 2
BF = jnp.bfloat16
F32 = jnp.float32
NT = (((1,), (1,)), ((), ()))
NN = (((1,), (0,)), ((), ()))


def grid_of(n_req):
    chips = n_req // CORES
    b = 1
    while b * 2 * b * 2 <= chips:
        b *= 2
    while chips % b:
        b -= 1
    return chips // b, b


def kernel(
    n_req, n_head, jn, cw,
    pages, own_len, queries, new_kv, man, resid, own_hbm, wo_hbm, wg_hbm, wu_hbm,
    out_ref, hid_ref,
    pool, wo, wg, wu, qf, qbuf, ksib, bias, nf, sbuf, rbuf, abuf, af, amat, dbuf,
    rf, rn, xb, pf, e1s, e1r, e2f, e2s, e2r, e3f, e3s, e3r,
    lsem, kv_s, kv_r, q_s, q_r, p_s, p_r, c_s, c_r, f_s, f_r, d_s, d_r,
    e1_ss, e1_rs, e2_ss, e2_rs, e3_ss, e3_rs,
):
    A, B = grid_of(n_req)
    NC = A * B
    kv = man.shape[2] // HD
    rows = queries.shape[0]
    blk = rows * GROUP
    width = wg.shape[1]
    scale = HD ** (-0.5)

    me = lax.axis_index("req")
    hd = lax.axis_index("head")
    core = lax.rem(me, CORES)
    chip = me // CORES
    a = chip // B
    b = lax.rem(chip, B)
    cp = b * A + a

    def dev(cp_, core_):
        return {"req": (lax.rem(cp_, A) * B + cp_ // A) * CORES + core_, "head": hd}

    def remote(src, dst, ss, rs, to):
        return pltpu.make_async_remote_copy(
            src_ref=src, dst_ref=dst, send_sem=ss, recv_sem=rs,
            device_id=to, device_id_type=pl.DeviceIdType.MESH,
        )

    sib = dev(cp, 1 - core)
    peers = [lax.rem(cp + i, NC) for i in range(NC)]
    froms = [lax.rem(cp + NC - i, NC) for i in range(NC)]

    barrier = pltpu.get_barrier_semaphore()

    def greet(to):
        pl.semaphore_signal(barrier, inc=1, device_id=to, device_id_type=pl.DeviceIdType.MESH)

    greet(sib)
    for i in range(1, NC):
        greet(dev(peers[i], core))
    for h in range(1, n_head):
        greet({"req": me, "head": lax.rem(hd + h, n_head)})

    loads = [
        pltpu.make_async_copy(own_hbm.at[0], pool.at[0], lsem.at[0]),
        pltpu.make_async_copy(own_hbm.at[1], pool.at[1], lsem.at[1]),
        pltpu.make_async_copy(wo_hbm, wo, lsem.at[2]),
        pltpu.make_async_copy(wg_hbm, wg, lsem.at[3]),
        pltpu.make_async_copy(wu_hbm, wu, lsem.at[4]),
    ]
    for c in loads:
        c.start()

    qv = queries[...].astype(F32)
    for k in range(kv):
        for g in range(GROUP):
            lane = (k * GROUP + g) * HD
            qf[pl.ds(k * blk + g, rows, stride=GROUP), :] = qv[:, lane:lane + HD]
    qbuf[cp] = qf[...].astype(BF)

    pl.semaphore_wait(barrier, 1 + (NC - 1) + (n_head - 1))

    kv_copy = remote(man, ksib, kv_s, kv_r, sib)
    kv_copy.start()
    q_out = [remote(qbuf.at[cp], qbuf.at[cp], q_s.at[i], q_r.at[i], dev(peers[i], core)) for i in range(1, NC)]
    for c in q_out:
        c.start()

    toks = pool.shape[1]
    tok_page = lax.broadcasted_iota(jnp.int32, (GROUP, toks), 1) // PAGE
    for r in range(rows):
        cnt = jnp.zeros((GROUP, toks), F32)
        for i in range(MAXP):
            pid = jnp.where(i < own_len[r], pages[r, i], -1)
            cnt = cnt + jnp.where(tok_page == pid, 1.0, 0.0)
        bias[r * GROUP:(r + 1) * GROUP, :] = jnp.where(cnt > 0.0, jnp.log(jnp.maximum(cnt, 1.0)), -1e30)
    for t in range(2):
        nv = new_kv[t].astype(F32)
        for k in range(kv):
            for g in range(GROUP):
                nf[t, pl.ds(k * blk + g, rows, stride=GROUP), :] = nv[:, k * HD:(k + 1) * HD]
    loads[0].wait()
    loads[1].wait()
    own = []
    for k in range(kv):
        rs = slice(k * blk, (k + 1) * blk)
        ls = slice(k * HD, (k + 1) * HD)
        s = lax.dot_general(qf[rs].astype(BF), pool[0, :, ls], NT, preferred_element_type=F32) * scale + bias[...]
        s_new = jnp.sum(qf[rs] * nf[0, rs], axis=1, keepdims=True) * scale
        m = jnp.maximum(jnp.max(s, axis=1, keepdims=True), s_new)
        p = jnp.exp(s - m)
        e_new = jnp.exp(s_new - m)
        l = jnp.sum(p, axis=1, keepdims=True) + e_new
        acc = lax.dot_general(p.astype(BF), pool[1, :, ls], NN, preferred_element_type=F32)
        acc = acc + e_new.astype(BF).astype(F32) * nf[1, rs]
        own.append((m, l, acc))

    kv_copy.wait()
    for i in range(1, NC):
        remote(qbuf.at[froms[i]], qbuf.at[froms[i]], q_s.at[i], q_r.at[i], dev(peers[i], core)).wait()
    lane = lax.broadcasted_iota(jnp.int32, (NC * blk, HD), 1)
    stats = jnp.zeros((NC * blk, HD), F32)
    for k in range(kv):
        ls = slice(k * HD, (k + 1) * HD)
        q = qbuf[:, k * blk:(k + 1) * blk, :].reshape(NC * blk, HD)
        s0 = lax.dot_general(q, man[0, :, ls], NT, preferred_element_type=F32) * scale
        s1 = lax.dot_general(q, ksib[0, :, ls], NT, preferred_element_type=F32) * scale
        m = jnp.maximum(jnp.max(s0, axis=1, keepdims=True), jnp.max(s1, axis=1, keepdims=True))
        m = m.astype(BF).astype(F32)
        p0 = jnp.exp(s0 - m)
        p1 = jnp.exp(s1 - m)
        l = jnp.sum(p0, axis=1, keepdims=True) + jnp.sum(p1, axis=1, keepdims=True)
        acc = lax.dot_general(p0.astype(BF), man[1, :, ls], NN, preferred_element_type=F32)
        acc = acc + lax.dot_general(p1.astype(BF), ksib[1, :, ls], NN, preferred_element_type=F32)
        sbuf[:, k * blk:(k + 1) * blk, :] = acc.astype(BF).reshape(NC, blk, HD)
        l_hi = l.astype(BF).astype(F32)
        stats = jnp.where(lane == k, m, stats)
        stats = jnp.where(lane == kv + k, l_hi, stats)
        stats = jnp.where(lane == 2 * kv + k, l - l_hi, stats)
    sbuf[:, kv * blk:(kv + 1) * blk, :] = stats.astype(BF).reshape(NC, blk, HD)
    p_out = [remote(sbuf.at[peers[i]], rbuf.at[cp], p_s.at[i], p_r.at[i], dev(peers[i], core)) for i in range(1, NC)]
    for c in p_out:
        c.start()
    rbuf[cp] = sbuf[cp]
    for i in range(1, NC):
        remote(sbuf.at[peers[i]], rbuf.at[froms[i]], p_s.at[i], p_r.at[i], dev(peers[i], core)).wait()

    st = [rbuf[n, kv * blk:(kv + 1) * blk, :].astype(F32) for n in range(NC)]
    mine = core * NC + cp
    for k in range(kv):
        rs = slice(k * blk, (k + 1) * blk)
        m, l, acc = own[k]
        top = m
        for n in range(NC):
            top = jnp.maximum(top, st[n][:, k:k + 1])
        f = jnp.exp(m - top)
        l = l * f
        acc = acc * f
        for n in range(NC):
            f = jnp.exp(st[n][:, k:k + 1] - top)
            l = l + f * (st[n][:, kv + k:kv + k + 1] + st[n][:, 2 * kv + k:2 * kv + k + 1])
            acc = acc + f * rbuf[n, rs, :].astype(F32)
        abuf[mine, rs, :] = (acc / l).astype(BF)
    slot = abuf.at[mine]
    fwd = [remote(slot, slot, f_s.at[0], f_r.at[0], sib)]
    fwd[0].start()
    c_out = [remote(slot, slot, c_s.at[i], c_r.at[i], dev(peers[i], core)) for i in range(1, NC)]
    for c in c_out:
        c.start()
    for i in range(1, NC):
        got = abuf.at[core * NC + froms[i]]
        remote(got, got, c_s.at[i], c_r.at[i], dev(peers[i], core)).wait_recv()
        c = remote(got, got, f_s.at[i], f_r.at[i], sib)
        c.start()
        fwd.append(c)

    rv = resid[...].astype(F32)
    order = [(ai * B + bi) * CORES + ci for ci in range(CORES) for bi in range(B) for ai in range(A)]
    for pos, nat in enumerate(order):
        rf[pos * rows:(pos + 1) * rows, :] = rv[nat * rows:(nat + 1) * rows, :]
    for i in range(NC):
        got = abuf.at[(1 - core) * NC + froms[i]]
        remote(got, got, f_s.at[i], f_r.at[i], sib).wait_recv()

    all_rows = n_req * rows
    for k in range(kv):
        af[k] = abuf[:, k * blk:(k + 1) * blk, :].astype(F32).reshape(n_req * blk, HD)
    for k in range(kv):
        for g in range(GROUP):
            lane0 = (k * GROUP + g) * HD
            amat[:, lane0:lane0 + HD] = af[k, pl.ds(g, all_rows, stride=GROUP), :].astype(BF)
    loads[2].wait()
    part = lax.dot_general(amat[...], wo[...], NN, preferred_element_type=F32)
    dbuf[hd] = part.astype(BF)
    d_out = []
    for h in range(1, n_head):
        to = {"req": me, "head": lax.rem(hd + h, n_head)}
        c = remote(dbuf.at[hd], dbuf.at[hd], d_s.at[h], d_r.at[h], to)
        c.start()
        d_out.append(c)
    for c in c_out:
        c.wait_send()
    for c in fwd:
        c.wait_send()
    loads[3].wait()
    loads[4].wait()
    for h in range(1, n_head):
        src = lax.rem(hd + n_head - h, n_head)
        remote(dbuf.at[src], dbuf.at[src], d_s.at[h], d_r.at[h], {"req": me, "head": lax.rem(hd + h, n_head)}).wait()
    total = dbuf[0].astype(F32)
    for h in range(1, n_head):
        total = total + dbuf[h].astype(F32)
    x = (rf[...] + total).astype(BF)
    xb[...] = x
    rf[...] = x.astype(F32)

    half = NC * rows
    quarter = A * rows
    lines = [lax.rem(a + i, A) for i in range(A)]
    line_from = [lax.rem(a + A - i, A) for i in range(A)]
    cols = [lax.rem(b + i, B) for i in range(B)]
    col_from = [lax.rem(b + B - i, B) for i in range(B)]

    def e1(j):
        return remote(e1s.at[j], e1r.at[j], e1_ss.at[j], e1_rs.at[j], sib)

    def e2(j, i):
        return remote(e2s.at[j, cols[i]], e2r.at[j, i], e2_ss.at[j, i], e2_rs.at[j, i], dev(cols[i] * A + a, core))

    def e3(j, i):
        return remote(e3s.at[j, lines[i]], e3r.at[j, i], e3_ss.at[j, i], e3_rs.at[j, i], dev(b * A + lines[i], core))

    def stage1(j):
        for q in range(4):
            w = wg if q < 2 else wu
            c0 = (q % 2) * (width // 2) + j * cw
            d = lax.dot_general(xb[...], w[:, c0:c0 + cw], NN, preferred_element_type=F32)
            pf[j, q] = d.reshape(CORES, half, cw)
        for q in range(4):
            e1s[j, q] = pf[j, q, 1 - core].astype(BF)
        e1(j).start()

    def stage2(j):
        e1(j).wait()
        for q in range(4):
            e2f[j, :, q] = (pf[j, q, core] + e1r[j, q].astype(F32)).reshape(B, quarter, cw)
        e2s[j] = e2f[j].astype(BF)
        for i in range(1, B):
            e2(j, i).start()

    def stage3(j):
        for i in range(1, B):
            e2(j, i).wait()
        for q in range(4):
            v = e2f[j, b, q]
            for i in range(1, B):
                v = v + e2r[j, i, q].astype(F32)
            for ai in range(A):
                e3f[j, ai, q * rows:(q + 1) * rows, :] = v[ai * rows:(ai + 1) * rows, :]
        e3s[j] = e3f[j].astype(BF)
        for i in range(1, A):
            e3(j, i).start()

    def stage4(j):
        for i in range(1, A):
            e3(j, i).wait()
        v = e3f[j, a]
        for i in range(1, A):
            v = v + e3r[j, i].astype(F32)
        gate = v[:2 * rows]
        up = v[2 * rows:]
        hid = (gate / (1.0 + jnp.exp(-gate)) * up).astype(BF)
        hid_ref[:, j * cw:(j + 1) * cw] = hid[:rows]
        hid_ref[:, width // 2 + j * cw:width // 2 + (j + 1) * cw] = hid[rows:]

    for t in range(jn + 3):
        if t < jn:
            stage1(t)
        if t == 0:
            for pos, nat in enumerate(order):
                rn[nat * rows:(nat + 1) * rows, :] = rf[pos * rows:(pos + 1) * rows, :]
            out_ref[...] = rn[...].astype(BF)
        if 0 <= t - 1 < jn:
            stage2(t - 1)
        if 0 <= t - 2 < jn:
            stage3(t - 2)
        if 0 <= t - 3 < jn:
            stage4(t - 3)


def on_device(n_req, n_head, queries, new_kv, own_kv, man_kv, pages, own_len, resid, w_out, w_gate, w_up):
    A, B = grid_of(n_req)
    NC = A * B
    rows = queries.shape[0]
    kv = new_kv.shape[2] // HD
    blk = rows * GROUP
    pool_t = own_kv.shape[1] * PAGE
    man_t = man_kv.shape[1] * PAGE
    width = w_gate.shape[1]
    cw = 896 if (width // 2) % 896 == 0 else width // 2
    jn = width // 2 // cw
    cols = resid.shape[1]
    all_rows = n_req * rows
    own = own_kv.reshape(2, pool_t, kv * HD)
    man = man_kv.reshape(2, man_t, kv * HD)
    V = pltpu.VMEM
    DMA = pltpu.SemaphoreType.DMA
    vm = pl.BlockSpec(memory_space=pltpu.VMEM)
    sm = pl.BlockSpec(memory_space=pltpu.SMEM)
    hb = pl.BlockSpec(memory_space=pl.ANY)
    quarter = A * rows
    scratch = [
        V((2, pool_t, kv * HD), BF), V(w_out.shape, BF), V(w_gate.shape, BF), V(w_up.shape, BF),
        V((kv * blk, HD), F32), V((NC, kv * blk, HD), BF), V((2, man_t, kv * HD), BF),
        V((blk, pool_t), F32), V((2, kv * blk, HD), F32),
        V((NC, (kv + 1) * blk, HD), BF), V((NC, (kv + 1) * blk, HD), BF),
        V((n_req, kv * blk, HD), BF), V((kv, n_req * blk, HD), F32), V((all_rows, kv * GROUP * HD), BF),
        V((n_head, all_rows, cols), BF), V((all_rows, cols), F32), V((all_rows, cols), F32), V((all_rows, cols), BF),
        V((jn, 4, CORES, NC * rows, cw), F32), V((jn, 4, NC * rows, cw), BF), V((jn, 4, NC * rows, cw), BF),
        V((jn, B, 4, quarter, cw), F32), V((jn, B, 4, quarter, cw), BF), V((jn, B, 4, quarter, cw), BF),
        V((jn, A, 4 * rows, cw), F32), V((jn, A, 4 * rows, cw), BF), V((jn, A, 4 * rows, cw), BF),
        DMA((5,)), DMA, DMA, DMA((NC,)), DMA((NC,)), DMA((NC,)), DMA((NC,)),
        DMA((NC,)), DMA((NC,)), DMA((NC,)), DMA((NC,)), DMA((n_head,)), DMA((n_head,)),
        DMA((jn,)), DMA((jn,)), DMA((jn, B)), DMA((jn, B)), DMA((jn, A)), DMA((jn, A)),
    ]
    return pl.pallas_call(
        functools.partial(kernel, n_req, n_head, jn, cw),
        out_shape=(
            jax.ShapeDtypeStruct((all_rows, cols), BF),
            jax.ShapeDtypeStruct((rows, width), BF),
        ),
        in_specs=[sm, sm, vm, vm, vm, vm, hb, hb, hb, hb],
        out_specs=(vm, vm),
        scratch_shapes=scratch,
        compiler_params=pltpu.CompilerParams(
            collective_id=0, has_side_effects=True, vmem_limit_bytes=58 * 1024 * 1024
        ),
        name="decode_layer",
    )(pages, own_len, queries, new_kv, man, resid, own, w_out, w_gate, w_up)


def solution(mesh):
    in_specs = (
        P("req", "head"),
        P(None, "req", "head"),
        P(None, "req", None, "head"),
        P(None, "req", None, "head"),
        P("req", None),
        P("req"),
        P(None, "req"),
        P("head", "req"),
        P("req", "head"),
        P("req", "head"),
    )
    out_specs = (P(None, "req"), P("req", "head"))
    return jax.shard_map(
        functools.partial(on_device, mesh.shape["req"], mesh.shape["head"]),
        mesh=mesh, in_specs=in_specs, out_specs=out_specs, check_vma=False,
    )
```

time: 247 us -> 60.6 us (0.25)
  waiting for transfers between devices: 160 us -> 0 us
  Pallas kernels: 0 us -> 56.8 us
  local copies, waits for them, and re-layouts: 28 us -> 2.93 us
  blocking collectives: 20.3 us -> 0 us
  matrix products: 17.6 us -> 0 us
  between operations: 14.5 us -> 0.64 us
  other arithmetic: 6.04 us -> 0 us
    unnamed x4 -> x0, waiting for transfers between devices: 106 us -> none
    pallas_call x0 -> x1, Pallas kernels: none -> 56.8 us  [on_device(): pl.pallas_call(functools.partial(kernel, n_req, n_head, jn, cw), out_shap...]
    all_gather x1 -> x0, waiting for transfers between devices: 36.2 us -> none  [on_device(): piece = lax.all_gather(man_kv, 'req', axis=1, tiled=True)]
    all_gather x1 -> x0, blocking collectives: 20.3 us -> none  [on_device(): lax.all_gather(attn, 'req', axis=0, tiled=True)]
    psum x1 -> x0, waiting for transfers between devices: 18.1 us -> none  [on_device(): lax.psum(partial_out.astype(jnp.bfloat16), 'head').astype(jnp.float32)]
    dot_general x8 -> x0, matrix products: 17.6 us -> none  [the longest x1 4.62 us: on_device(): gate_part = jnp.dot(resid_out, w_gate, preferred_element_type=jnp.float32)]
    gather x2 -> x0, local copies, waits for them, and re-layouts: 7.65 us -> none  [on_device(): picked = own_kv[:, pages].reshape(2, rows, MAXP * PAGE, kv_dev, HD)]
    squeeze x3 -> x0, local copies, waits for them, and re-layouts: 6.18 us -> none  [the longest x1 4.09 us: on_device(): picked[0]]
  transfers between devices with their start and end apart: 3 -> 0, of which waited for: 3 -> 0; matrix products, arithmetic and copies ran while one was open for 8% -> 0% of each run, Pallas kernels for 0% -> 0%
where the time goes in v1:
time: 60.6 us; the launch traced here: 60.4 us
  Pallas kernels  56.8 us (94%)
  local copies, waits for them, and re-layouts  2.93 us (5%)
  between operations  0.64 us (1%)
    pallas_call x1, Pallas kernels, on_device(): pl.pallas_call(functools.partial(kernel, n_req, n_head, jn, cw), out_shap...  56.8 us
    unnamed x2, local copies, waits for them, and re-layouts  2.93 us

profile of v1, /device:TPU:0, one launch (start us, length us, event | category | flops | bytes accessed | tf_op | source)
XLA Modules:
  0.0 60.4 jit_solution(9571759318818874771)
XLA Ops:
  0.6 56.8 %decode_layer.1 = (bf16[64,512]{1,0:T(8,128)(2,1)}, bf16[4,7168]{1,0:T(4,128)(2,1)}) custom-call(s32[4,8]{1,0:T(4,128)} %pages.1, s32[4]{0:T(128)} %own_len.1, bf16[4,4096]{1,0:T(4,128)(2,1)} %queries.1, bf16[2,4,512]{2,1,0:T(4,128)(2,1)} %new_kv.1, bf16[2,128,512]{2,1,0:T(8,128)(2,1)} %bitcast.3, bf16[64,512]{1,0:T(8,128)(2,1)} %resid.1, ...), custom_call_target="tpu_custom_call" | custom-call | tf_op jit(solution)/shard_map/decode_layer/pallas_call | solution.py:342
  57.4 1.5 %copy.14 = bf16[64,512]{1,0:T(8,128)(2,1)} copy(bf16[64,512]{1,0:T(8,128)(2,1)} %get-tuple-element.4) | data formatting | bytes 131072
  58.9 1.5 %copy.15 = bf16[4,7168]{1,0:T(4,128)(2,1)} copy(bf16[4,7168]{1,0:T(4,128)(2,1)} %get-tuple-element.5) | data formatting | bytes 114688

commit v2 on v1

--- a/solution.py
+++ b/solution.py
@@ -30,11 +30,11 @@
 
 def kernel(
     n_req, n_head, jn, cw,
-    pages, own_len, queries, new_kv, man, resid, own_hbm, wo_hbm, wg_hbm, wu_hbm,
+    pages, own_len, queries, new_kv, man, res_hbm, own_hbm, wo_hbm, wg_hbm, wu_hbm,
     out_ref, hid_ref,
-    pool, wo, wg, wu, qf, qbuf, ksib, bias, nf, sbuf, rbuf, abuf, af, amat, dbuf,
+    pool, wo, wg, wu, qf, qbuf, kvb, resid, bias, nf, sbuf, rbuf, abuf, af, amat, dbuf,
     rf, rn, xb, pf, e1s, e1r, e2f, e2s, e2r, e3f, e3s, e3r,
-    lsem, kv_s, kv_r, q_s, q_r, p_s, p_r, c_s, c_r, f_s, f_r, d_s, d_r,
+    lsem, kv_s, kv_r, kf_s, kf_r, q_s, q_r, p_s, p_r, c_s, c_r, y_s, y_r, f_s, f_r, d_s, d_r,
     e1_ss, e1_rs, e2_ss, e2_rs, e3_ss, e3_rs,
 ):
     A, B = grid_of(n_req)
@@ -63,8 +63,14 @@
         )
 
     sib = dev(cp, 1 - core)
-    peers = [lax.rem(cp + i, NC) for i in range(NC)]
-    froms = [lax.rem(cp + NC - i, NC) for i in range(NC)]
+    lines = [lax.rem(a + i, A) for i in range(A)]
+    line_from = [lax.rem(a + A - i, A) for i in range(A)]
+    cols = [lax.rem(b + i, B) for i in range(B)]
+    col_from = [lax.rem(b + B - i, B) for i in range(B)]
+    line_dev = [dev(b * A + lines[i], core) for i in range(A)]
+    col_dev = [dev(cols[i] * A + a, core) for i in range(B)]
+    parts = [(0, kv // 2), (kv // 2, kv)] if kv > 1 else [(0, kv)]
+    np_ = len(parts)
 
     barrier = pltpu.get_barrier_semaphore()
 
@@ -72,8 +78,10 @@
         pl.semaphore_signal(barrier, inc=1, device_id=to, device_id_type=pl.DeviceIdType.MESH)
 
     greet(sib)
-    for i in range(1, NC):
-        greet(dev(peers[i], core))
+    for i in range(1, A):
+        greet(line_dev[i])
+    for i in range(1, B):
+        greet(col_dev[i])
     for h in range(1, n_head):
         greet({"req": me, "head": lax.rem(hd + h, n_head)})
 
@@ -83,24 +91,48 @@
         pltpu.make_async_copy(wo_hbm, wo, lsem.at[2]),
         pltpu.make_async_copy(wg_hbm, wg, lsem.at[3]),
         pltpu.make_async_copy(wu_hbm, wu, lsem.at[4]),
+        pltpu.make_async_copy(man, kvb.at[b, core], lsem.at[5]),
+        pltpu.make_async_copy(res_hbm, resid, lsem.at[6]),
     ]
-    for c in loads:
-        c.start()
+    loads[0].start()
+    loads[1].start()
 
     qv = queries[...].astype(F32)
     for k in range(kv):
         for g in range(GROUP):
             lane = (k * GROUP + g) * HD
             qf[pl.ds(k * blk + g, rows, stride=GROUP), :] = qv[:, lane:lane + HD]
-    qbuf[cp] = qf[...].astype(BF)
-
-    pl.semaphore_wait(barrier, 1 + (NC - 1) + (n_head - 1))
-
-    kv_copy = remote(man, ksib, kv_s, kv_r, sib)
-    kv_copy.start()
-    q_out = [remote(qbuf.at[cp], qbuf.at[cp], q_s.at[i], q_r.at[i], dev(peers[i], core)) for i in range(1, NC)]
-    for c in q_out:
-        c.start()
+    qbuf[a] = qf[...].astype(BF)
+
+    pl.semaphore_wait(barrier, 1 + (A - 1) + (B - 1) + (n_head - 1))
+
+    def kv_col(t, i):
+        return remote(man.at[t], kvb.at[b, core, t], kv_s.at[t, i], kv_r.at[t, i], col_dev[i])
+
+    def kv_sib(t, i):
+        src = man.at[t] if i == 0 else kvb.at[col_from[i], core, t]
+        return remote(src, kvb.at[col_from[i], core, t], kf_s.at[t, i], kf_r.at[t, i], sib)
+
+    def q_line(i):
+        return remote(qbuf.at[a], qbuf.at[a], q_s.at[i], q_r.at[i], line_dev[i])
+
+    for i in range(1, B):
+        kv_col(0, i).start()
+    for i in range(1, A):
+        q_line(i).start()
+    for i in range(1, B):
+        kv_col(1, i).start()
+    kv_sib(0, 0).start()
+    kv_sib(1, 0).start()
+    loads[5].start()
+    loads[6].start()
+
+    def kv_forward(t):
+        for i in range(1, B):
+            kv_col(t, i).wait_send()
+            got = kvb.at[col_from[i], core, t]
+            remote(got, got, kv_s.at[t, i], kv_r.at[t, i], col_dev[i]).wait_recv()
+            kv_sib(t, i).start()
 
     toks = pool.shape[1]
     tok_page = lax.broadcasted_iota(jnp.int32, (GROUP, toks), 1) // PAGE
@@ -117,6 +149,8 @@
                 nf[t, pl.ds(k * blk + g, rows, stride=GROUP), :] = nv[:, k * HD:(k + 1) * HD]
     loads[0].wait()
     loads[1].wait()
+    for c in loads[2:5]:
+        c.start()
     own = []
     for k in range(kv):
         rs = slice(k * blk, (k + 1) * blk)
@@ -130,83 +164,135 @@
         acc = lax.dot_general(p.astype(BF), pool[1, :, ls], NN, preferred_element_type=F32)
         acc = acc + e_new.astype(BF).astype(F32) * nf[1, rs]
         own.append((m, l, acc))
-
-    kv_copy.wait()
-    for i in range(1, NC):
-        remote(qbuf.at[froms[i]], qbuf.at[froms[i]], q_s.at[i], q_r.at[i], dev(peers[i], core)).wait()
-    lane = lax.broadcasted_iota(jnp.int32, (NC * blk, HD), 1)
-    stats = jnp.zeros((NC * blk, HD), F32)
-    for k in range(kv):
-        ls = slice(k * HD, (k + 1) * HD)
-        q = qbuf[:, k * blk:(k + 1) * blk, :].reshape(NC * blk, HD)
-        s0 = lax.dot_general(q, man[0, :, ls], NT, preferred_element_type=F32) * scale
-        s1 = lax.dot_general(q, ksib[0, :, ls], NT, preferred_element_type=F32) * scale
-        m = jnp.maximum(jnp.max(s0, axis=1, keepdims=True), jnp.max(s1, axis=1, keepdims=True))
-        m = m.astype(BF).astype(F32)
-        p0 = jnp.exp(s0 - m)
-        p1 = jnp.exp(s1 - m)
-        l = jnp.sum(p0, axis=1, keepdims=True) + jnp.sum(p1, axis=1, keepdims=True)
-        acc = lax.dot_general(p0.astype(BF), man[1, :, ls], NN, preferred_element_type=F32)
-        acc = acc + lax.dot_general(p1.astype(BF), ksib[1, :, ls], NN, preferred_element_type=F32)
-        sbuf[:, k * blk:(k + 1) * blk, :] = acc.astype(BF).reshape(NC, blk, HD)
-        l_hi = l.astype(BF).astype(F32)
-        stats = jnp.where(lane == k, m, stats)
-        stats = jnp.where(lane == kv + k, l_hi, stats)
-        stats = jnp.where(lane == 2 * kv + k, l - l_hi, stats)
-    sbuf[:, kv * blk:(kv + 1) * blk, :] = stats.astype(BF).reshape(NC, blk, HD)
-    p_out = [remote(sbuf.at[peers[i]], rbuf.at[cp], p_s.at[i], p_r.at[i], dev(peers[i], core)) for i in range(1, NC)]
-    for c in p_out:
+        if k == (kv - 1) // 2:
+            kv_forward(0)
+    kv_forward(1)
+
+    loads[5].wait()
+    for i in range(1, A):
+        q_line(i).wait_send()
+        got = qbuf.at[line_from[i]]
+        remote(got, got, q_s.at[i], q_r.at[i], line_dev[i]).wait_recv()
+    for t in range(2):
+        for i in range(B):
+            kv_sib(t, i).wait_send()
+            got = kvb.at[col_from[i], 1 - core, t]
+            remote(got, got, kf_s.at[t, i], kf_r.at[t, i], sib).wait_recv()
+    mrows = A * blk
+    mtoks = B * CORES * kvb.shape[3]
+    lane = lax.broadcasted_iota(jnp.int32, (mrows, HD), 1)
+    stats = jnp.zeros((mrows, HD), F32)
+
+    def p_line(n, i):
+        r0, r1 = parts[n][0] * blk, parts[n][1] * blk + (blk if n == np_ - 1 else 0)
+        return remote(
+            sbuf.at[lines[i], r0:r1], rbuf.at[a, r0:r1], p_s.at[n, i], p_r.at[n, i], line_dev[i]
+        )
+
+    def p_wait(n, i):
+        r0, r1 = parts[n][0] * blk, parts[n][1] * blk + (blk if n == np_ - 1 else 0)
+        p_line(n, i).wait_send()
+        got = rbuf.at[line_from[i], r0:r1]
+        remote(got, got, p_s.at[n, i], p_r.at[n, i], line_dev[i]).wait_recv()
+
+    for n, (k0, k1) in enumerate(parts):
+        for k in range(k0, k1):
+            ls = slice(k * HD, (k + 1) * HD)
+            q = qbuf[:, k * blk:(k + 1) * blk, :].reshape(mrows, HD)
+            keys = kvb[:, :, 0, :, ls].reshape(mtoks, HD)
+            vals = kvb[:, :, 1, :, ls].reshape(mtoks, HD)
+            s = lax.dot_general(q, keys, NT, preferred_element_type=F32) * scale
+            m = jnp.max(s, axis=1, keepdims=True).astype(BF).astype(F32)
+            p = jnp.exp(s - m)
+            l = jnp.sum(p, axis=1, keepdims=True)
+            acc = lax.dot_general(p.astype(BF), vals, NN, preferred_element_type=F32)
+            sbuf[:, k * blk:(k + 1) * blk, :] = acc.astype(BF).reshape(A, blk, HD)
+            l_hi = l.astype(BF).astype(F32)
+            stats = jnp.where(lane == k, m, stats)
+            stats = jnp.where(lane == kv + k, l_hi, stats)
+            stats = jnp.where(lane == 2 * kv + k, l - l_hi, stats)
+        if n == np_ - 1:
+            sbuf[:, kv * blk:(kv + 1) * blk, :] = stats.astype(BF).reshape(A, blk, HD)
+        for i in range(1, A):
+            p_line(n, i).start()
+    rbuf[a] = sbuf[a]
+    for n in range(np_):
+        for i in range(1, A):
+            p_wait(n, i)
+
+    st = [rbuf[n, kv * blk:(kv + 1) * blk, :].astype(F32) for n in range(A)]
+    mine = core * NC + cp
+    sends = []
+
+    def push(n, slot, ss, rs, to):
+        ref = abuf.at[slot, parts[n][0] * blk:parts[n][1] * blk]
+        c = remote(ref, ref, ss, rs, to)
         c.start()
-    rbuf[cp] = sbuf[cp]
-    for i in range(1, NC):
-        remote(sbuf.at[peers[i]], rbuf.at[froms[i]], p_s.at[i], p_r.at[i], dev(peers[i], core)).wait()
-
-    st = [rbuf[n, kv * blk:(kv + 1) * blk, :].astype(F32) for n in range(NC)]
-    mine = core * NC + cp
-    for k in range(kv):
-        rs = slice(k * blk, (k + 1) * blk)
-        m, l, acc = own[k]
-        top = m
-        for n in range(NC):
-            top = jnp.maximum(top, st[n][:, k:k + 1])
-        f = jnp.exp(m - top)
-        l = l * f
-        acc = acc * f
-        for n in range(NC):
-            f = jnp.exp(st[n][:, k:k + 1] - top)
-            l = l + f * (st[n][:, kv + k:kv + k + 1] + st[n][:, 2 * kv + k:2 * kv + k + 1])
-            acc = acc + f * rbuf[n, rs, :].astype(F32)
-        abuf[mine, rs, :] = (acc / l).astype(BF)
-    slot = abuf.at[mine]
-    fwd = [remote(slot, slot, f_s.at[0], f_r.at[0], sib)]
-    fwd[0].start()
-    c_out = [remote(slot, slot, c_s.at[i], c_r.at[i], dev(peers[i], core)) for i in range(1, NC)]
-    for c in c_out:
-        c.start()
-    for i in range(1, NC):
-        got = abuf.at[core * NC + froms[i]]
-        remote(got, got, c_s.at[i], c_r.at[i], dev(peers[i], core)).wait_recv()
-        c = remote(got, got, f_s.at[i], f_r.at[i], sib)
-        c.start()
-        fwd.append(c)
-
+        sends.append(c)
+
+    def landed(n, slot, ss, rs, to):
+        ref = abuf.at[slot, parts[n][0] * blk:parts[n][1] * blk]
+        remote(ref, ref, ss, rs, to).wait_recv()
+
+    def slot_of(core_, ib, ia):
+        return core_ * NC + col_from[ib] * A + line_from[ia]
+
+    for n, (k0, k1) in enumerate(parts):
+        for k in range(k0, k1):
+            rs = slice(k * blk, (k + 1) * blk)
+            m, l, acc = own[k]
+            top = m
+            for i in range(A):
+                top = jnp.maximum(top, st[i][:, k:k + 1])
+            f = jnp.exp(m - top)
+            l = l * f
+            acc = acc * f
+            for i in range(A):
+                f = jnp.exp(st[i][:, k:k + 1] - top)
+                l = l + f * (st[i][:, kv + k:kv + k + 1] + st[i][:, 2 * kv + k:2 * kv + k + 1])
+                acc = acc + f * rbuf[i, rs, :].astype(F32)
+            abuf[mine, rs, :] = (acc / l).astype(BF)
+        for i in range(1, A):
+            push(n, mine, c_s.at[n, i], c_r.at[n, i], line_dev[i])
+        for i in range(1, B):
+            push(n, mine, y_s.at[n, i, 0], y_r.at[n, i, 0], col_dev[i])
+        push(n, mine, f_s.at[n, 0, 0], f_r.at[n, 0, 0], sib)
+    for n in range(np_):
+        for ia in range(1, A):
+            slot = slot_of(core, 0, ia)
+            landed(n, slot, c_s.at[n, ia], c_r.at[n, ia], line_dev[ia])
+            for ib in range(1, B):
+                push(n, slot, y_s.at[n, ib, ia], y_r.at[n, ib, ia], col_dev[ib])
+            push(n, slot, f_s.at[n, 0, ia], f_r.at[n, 0, ia], sib)
+    for n in range(np_):
+        for ib in range(1, B):
+            for ia in range(A):
+                slot = slot_of(core, ib, ia)
+                landed(n, slot, y_s.at[n, ib, ia], y_r.at[n, ib, ia], col_dev[ib])
+                push(n, slot, f_s.at[n, ib, ia], f_r.at[n, ib, ia], sib)
+
+    loads[6].wait()
     rv = resid[...].astype(F32)
     order = [(ai * B + bi) * CORES + ci for ci in range(CORES) for bi in range(B) for ai in range(A)]
     for pos, nat in enumerate(order):
         rf[pos * rows:(pos + 1) * rows, :] = rv[nat * rows:(nat + 1) * rows, :]
-    for i in range(NC):
-        got = abuf.at[(1 - core) * NC + froms[i]]
-        remote(got, got, f_s.at[i], f_r.at[i], sib).wait_recv()
 
     all_rows = n_req * rows
-    for k in range(kv):
-        af[k] = abuf[:, k * blk:(k + 1) * blk, :].astype(F32).reshape(n_req * blk, HD)
-    for k in range(kv):
-        for g in range(GROUP):
-            lane0 = (k * GROUP + g) * HD
-            amat[:, lane0:lane0 + HD] = af[k, pl.ds(g, all_rows, stride=GROUP), :].astype(BF)
     loads[2].wait()
-    part = lax.dot_general(amat[...], wo[...], NN, preferred_element_type=F32)
+    part = None
+    for n, (k0, k1) in enumerate(parts):
+        for ib in range(B):
+            for ia in range(A):
+                landed(n, slot_of(1 - core, ib, ia), f_s.at[n, ib, ia], f_r.at[n, ib, ia], sib)
+        for k in range(k0, k1):
+            af[k] = abuf[:, k * blk:(k + 1) * blk, :].astype(F32).reshape(n_req * blk, HD)
+        for k in range(k0, k1):
+            for g in range(GROUP):
+                lane0 = (k * GROUP + g) * HD
+                amat[:, lane0:lane0 + HD] = af[k, pl.ds(g, all_rows, stride=GROUP), :].astype(BF)
+        ks = slice(k0 * GROUP * HD, k1 * GROUP * HD)
+        d = lax.dot_general(amat[:, ks], wo[ks], NN, preferred_element_type=F32)
+        part = d if part is None else part + d
     dbuf[hd] = part.astype(BF)
     d_out = []
     for h in range(1, n_head):
@@ -214,9 +300,7 @@
         c = remote(dbuf.at[hd], dbuf.at[hd], d_s.at[h], d_r.at[h], to)
         c.start()
         d_out.append(c)
-    for c in c_out:
-        c.wait_send()
-    for c in fwd:
+    for c in sends:
         c.wait_send()
     loads[3].wait()
     loads[4].wait()
@@ -232,11 +316,6 @@
 
     half = NC * rows
     quarter = A * rows
-    lines = [lax.rem(a + i, A) for i in range(A)]
-    line_from = [lax.rem(a + A - i, A) for i in range(A)]
-    cols = [lax.rem(b + i, B) for i in range(B)]
-    col_from = [lax.rem(b + B - i, B) for i in range(B)]
-
     def e1(j):
         return remote(e1s.at[j], e1r.at[j], e1_ss.at[j], e1_rs.at[j], sib)
 
@@ -325,18 +404,20 @@
     sm = pl.BlockSpec(memory_space=pltpu.SMEM)
     hb = pl.BlockSpec(memory_space=pl.ANY)
     quarter = A * rows
+    np_ = 2 if kv > 1 else 1
     scratch = [
         V((2, pool_t, kv * HD), BF), V(w_out.shape, BF), V(w_gate.shape, BF), V(w_up.shape, BF),
-        V((kv * blk, HD), F32), V((NC, kv * blk, HD), BF), V((2, man_t, kv * HD), BF),
+        V((kv * blk, HD), F32), V((A, kv * blk, HD), BF), V((B, CORES, 2, man_t, kv * HD), BF), V((all_rows, cols), BF),
         V((blk, pool_t), F32), V((2, kv * blk, HD), F32),
-        V((NC, (kv + 1) * blk, HD), BF), V((NC, (kv + 1) * blk, HD), BF),
+        V((A, (kv + 1) * blk, HD), BF), V((A, (kv + 1) * blk, HD), BF),
         V((n_req, kv * blk, HD), BF), V((kv, n_req * blk, HD), F32), V((all_rows, kv * GROUP * HD), BF),
         V((n_head, all_rows, cols), BF), V((all_rows, cols), F32), V((all_rows, cols), F32), V((all_rows, cols), BF),
         V((jn, 4, CORES, NC * rows, cw), F32), V((jn, 4, NC * rows, cw), BF), V((jn, 4, NC * rows, cw), BF),
         V((jn, B, 4, quarter, cw), F32), V((jn, B, 4, quarter, cw), BF), V((jn, B, 4, quarter, cw), BF),
         V((jn, A, 4 * rows, cw), F32), V((jn, A, 4 * rows, cw), BF), V((jn, A, 4 * rows, cw), BF),
-        DMA((5,)), DMA, DMA, DMA((NC,)), DMA((NC,)), DMA((NC,)), DMA((NC,)),
-        DMA((NC,)), DMA((NC,)), DMA((NC,)), DMA((NC,)), DMA((n_head,)), DMA((n_head,)),
+        DMA((7,)), DMA((2, B)), DMA((2, B)), DMA((2, B)), DMA((2, B)), DMA((A,)), DMA((A,)),
+        DMA((np_, A)), DMA((np_, A)), DMA((np_, A)), DMA((np_, A)),
+        DMA((np_, B, A)), DMA((np_, B, A)), DMA((np_, B, A)), DMA((np_, B, A)), DMA((n_head,)), DMA((n_head,)),
         DMA((jn,)), DMA((jn,)), DMA((jn, B)), DMA((jn, B)), DMA((jn, A)), DMA((jn, A)),
     ]
     return pl.pallas_call(
@@ -345,7 +426,7 @@
             jax.ShapeDtypeStruct((all_rows, cols), BF),
             jax.ShapeDtypeStruct((rows, width), BF),
         ),
-        in_specs=[sm, sm, vm, vm, vm, vm, hb, hb, hb, hb],
+        in_specs=[sm, sm, vm, vm, hb, hb, hb, hb, hb, hb],
         out_specs=(vm, vm),
         scratch_shapes=scratch,
         compiler_params=pltpu.CompilerParams(

time: 60.6 us -> 59.2 us (0.977)
  Pallas kernels: 56.8 us -> 55.3 us
    pallas_call x1, Pallas kernels: 56.8 us -> 55.3 us  [on_device(): pl.pallas_call(functools.partial(kernel, n_req, n_head, jn, cw), out_shap...]
where the time goes in v2:
time: 59.2 us; the launch traced here: 58.9 us
  Pallas kernels  55.3 us (93%)
  local copies, waits for them, and re-layouts  2.93 us (5%)
  between operations  0.64 us (1%)
    pallas_call x1, Pallas kernels, on_device(): pl.pallas_call(functools.partial(kernel, n_req, n_head, jn, cw), out_shap...  55.3 us
    unnamed x2, local copies, waits for them, and re-layouts  2.93 us

profile of v2, /device:TPU:0, one launch (start us, length us, event | category | flops | bytes accessed | tf_op | source)
XLA Modules:
  0.0 58.9 jit_solution(9749467294579895330)
XLA Ops:
  0.6 55.3 %decode_layer.1 = (bf16[64,512]{1,0:T(8,128)(2,1)}, bf16[4,7168]{1,0:T(4,128)(2,1)}) custom-call(s32[4,8]{1,0:T(4,128)} %pages.1, s32[4]{0:T(128)} %own_len.1, bf16[4,4096]{1,0:T(4,128)(2,1)} %queries.1, bf16[2,4,512]{2,1,0:T(4,128)(2,1)} %new_kv.1, bf16[2,128,512]{2,1,0:T(8,128)(2,1)} %bitcast.3, bf16[64,512]{1,0:T(8,128)(2,1)} %res_hbm.1, ...), custom_call_target="tpu_custom_call" | custom-call | tf_op jit(solution)/shard_map/decode_layer/pallas_call | solution.py:423
  55.9 1.5 %copy.14 = bf16[64,512]{1,0:T(8,128)(2,1)} copy(bf16[64,512]{1,0:T(8,128)(2,1)} %get-tuple-element.4) | data formatting | bytes 131072
  57.4 1.5 %copy.15 = bf16[4,7168]{1,0:T(4,128)(2,1)} copy(bf16[4,7168]{1,0:T(4,128)(2,1)} %get-tuple-element.5) | data formatting | bytes 114688
